TPU v7x, 128 devices: a whole 4x4x4 slice. The times are simulated.
128 devices in a mesh: radial: 32 (over z, y_lo, x), chan: 4 (over y_hi, core).
Axes of the slice: x: 4, y: 4 (y_hi: 2, y_lo: 2; y = y_hi * 2 + y_lo), z: 4, core: 2. Of those that a mesh axis runs over, the one named last changes fastest.
Arguments:
- amplitudes: bfloat16 [256, 2048, 256], P('radial', 'chan'), may hold values from -6 to 6
- previous: bfloat16 [256, 2048, 256], P('radial', 'chan'), may hold values from -6 to 6
- coupling: bfloat16 [256, 2048, 2048], P('radial', 'chan'), may hold values from -0.125 to 0.125
- thresholds: float32 [2048], P('chan'), may hold values from 0 to 2
- barrier: float32 [2048], P('chan'), may hold values from 0.5 to 4
- block_order: int32 [16], replicated, may hold values from 0 to 15, each once
- window_offset: int32 [1], replicated, may hold values from 0 to 7936
Outputs:
- filtered: bfloat16 [256, 2048, 256], P('radial', 'chan')
Inputs may be any that keep to these rules, and one draw needn't show every extreme that they name: `block_order`: each of 0 to 15 once.
All inputs are finite; a program needn't handle non-finite values.
Results may differ from a plain program's by a relative error of at most 0.001.
Values may be sent and summed in bfloat16 or wider, within the bound.
A program may use at most 256 MiB of HBM per device.

v0:
```python
import jax
import jax.numpy as jnp
from jax import lax
from jax.sharding import PartitionSpec as P

CHB = 128
GRID = 8192


stencil_weights = (
    -1.0 / 560,
    8.0 / 315,
    -1.0 / 5,
    8.0 / 5,
    -205.0 / 72,
    8.0 / 5,
    -1.0 / 5,
    8.0 / 315,
    -1.0 / 560,
)


def from_behind(block, axis, distance):
    devices = range(lax.axis_size(axis))
    route = [((i - distance) % len(devices), i) for i in devices]
    return lax.ppermute(block, axis, route)


def padded_2(cells, sides, width):
    for axis, dim in sides:
        count = lax.axis_size(axis)
        ends = count - 1
        head = lax.slice_in_dim(cells, 0, width, axis=dim)
        tail = lax.slice_in_dim(cells, cells.shape[dim] - width, cells.shape[dim], axis=dim)
        cells = jnp.concatenate(
            [
                lax.ppermute(tail, axis, [(i, (i + 1) % count) for i in range(ends)]),
                cells,
                lax.ppermute(head, axis, [((i + 1) % count, i) for i in range(ends)]),
            ],
            axis=dim,
        )
    return cells


def local(amplitudes, previous, coupling, thresholds, barrier, block_order, window_offset):
    points = amplitudes.shape[0]
    local_rows = amplitudes.shape[1]
    blocks = block_order.shape[0]
    inverse = jnp.sum(
        jnp.arange(blocks, dtype=jnp.int32)[:, None]
        * (block_order[:, None] == jnp.arange(blocks, dtype=jnp.int32)[None, :]).astype(jnp.int32),
        axis=0,
    )
    blocked = coupling.reshape(points, local_rows, blocks, CHB)

    def product_part(piece, start):
        piece_blocks = piece.shape[1] // CHB
        first_block = start // CHB
        total = jnp.zeros((points, local_rows, piece.shape[2]), jnp.float32)
        for inner in range(piece_blocks):
            column_block = inverse[first_block + inner]
            matrices = lax.dynamic_slice_in_dim(blocked, column_block, 1, 2)[:, :, 0, :]
            vectors = piece[:, inner * CHB : (inner + 1) * CHB, :]
            total = total + jnp.einsum(
                "prm,pmk->prk", matrices, vectors, preferred_element_type=jnp.float32
            )
        return total

    ranking = lax.axis_index("chan")
    width_chan = lax.axis_size("chan")
    potential = product_part(amplitudes, ranking * local_rows)
    visitor = amplitudes
    for rotation in range(1, width_chan):
        visitor = from_behind(visitor, "chan", 1)
        source = (ranking - rotation) % width_chan
        potential = potential + product_part(visitor, source * local_rows)
    padded = padded_2(amplitudes, (("radial", 0),), 4)
    laplace = jnp.zeros(amplitudes.shape, jnp.float32)
    for shift_index in range(9):
        laplace = laplace + stencil_weights[shift_index] * padded[
            shift_index : shift_index + points
        ].astype(jnp.float32)
    first_point = lax.axis_index("radial") * points
    radius = (window_offset[0] + first_point + jnp.arange(points, dtype=jnp.int32) + 1).astype(
        jnp.float32
    ) / (GRID // 16)
    diagonal = thresholds[None, :] + barrier[None, :] / (1.0 + radius[:, None] ** 2)
    current = amplitudes.astype(jnp.float32)
    applied = -0.5 * laplace + diagonal[:, :, None] * current + potential
    result = 2.0 * (applied - 1.0 * current) / 6.0 - previous.astype(jnp.float32)
    return result.astype(jnp.bfloat16)


def solution(mesh):
    placed = (
        P("radial", "chan", None),
        P("radial", "chan", None),
        P("radial", "chan", None),
        P("chan"),
        P("chan"),
        P(),
        P(),
    )
    return jax.shard_map(
        local, mesh=mesh, in_specs=placed, out_specs=P("radial", "chan", None), check_vma=False
    )
```

profile of v0, /device:TPU:97, one launch (start us, length us, event | category | flops | bytes accessed | tf_op | source)
XLA Modules:
  0.0 211.8 jit_solution(10804442942773727394)
XLA Ops:
  0.0 3.5 %collective-permute-start.2 = (bf16[8,512,256]{2,1,0:T(8,128)(2,1)}, bf16[8,512,256]{2,1,0:T(8,128)(2,1)}, u32[]{:S(2)}, u32[]{:S(2)}) collective-permute-start(bf16[8,512,256]{2,1,0:T(8,128)(2,1)} %param.7), channel_id=1, source_target_pairs={{3,0},{0,1},{1,2},{2,3},{7,4},{4,5},{5,6},{6,7},{11,8},{8,9},{9,10... | collective-permute-start | bytes 6291464 | tf_op jit(solution)/shard_map/ppermute | solution.py:26
  3.5 3.0 %fusion.43 = (bf16[4,512,256]{2,1,0:T(8,128)(2,1)}, bf16[4,512,256]{2,1,0:T(8,128)(2,1)}) fusion(bf16[8,512,256]{2,1,0:T(8,128)(2,1)} %param.7), kind=kLoop, calls=%fused_computation.86 | loop fusion | bytes 4194304 | tf_op jit(solution)/shard_map/slice | solution.py:34
  6.5 3.1 %collective-permute-start = (bf16[4,512,256]{2,1,0:T(8,128)(2,1)}, bf16[4,512,256]{2,1,0:T(8,128)(2,1)}, u32[]{:S(2)}, u32[]{:S(2)}) collective-permute-start(bf16[4,512,256]{2,1,0:T(8,128)(2,1)} %get-tuple-element.23), channel_id=1, source_target_pairs={{0,4},{4,8},{8,12},{12,16},{16,20},{20,24},{24,28},{28,32},{32,36}... | collective-permute-start | bytes 3145736 | tf_op jit(solution)/shard_map/ppermute | solution.py:37
  9.6 5.2 %collective-permute-start.1 = (bf16[4,512,256]{2,1,0:T(8,128)(2,1)}, bf16[4,512,256]{2,1,0:T(8,128)(2,1)S(1)}, u32[]{:S(2)}, u32[]{:S(2)}) collective-permute-start(bf16[4,512,256]{2,1,0:T(8,128)(2,1)} %get-tuple-element.24), channel_id=1, source_target_pairs={{4,0},{8,4},{12,8},{16,12},{20,16},{24,20},{28,24},{32,28},{36,32}... | collective-permute-start | bytes 3145736 | tf_op jit(solution)/shard_map/ppermute | solution.py:39
  14.9 0.0 copy-done.21
  15.0 0.1 select_reduce_fusion
  15.1 0.8 fusion.44
  36.4 15.1 %copy.56 = bf16[512,8,16,128]{3,2,1,0:T(8,128)(2,1)} copy(bf16[512,8,16,128]{3,1,2,0:T(8,128)(2,1)} %bitcast.73) | data formatting | bytes 33554432
  61.7 0.0 copy-start
  61.7 57.9 %constant_dynamic-slice_fusion.15 = (bf16[8,512,1,128]{3,2,1,0:T(2,128)(2,1)}, bf16[8,512,1,128]{3,2,1,0:T(2,128)(2,1)}, bf16[8,512,1,128]{3,2,1,0:T(2,128)(2,1)...) fusion(bf16[8,512,16,128]{3,2,1,0:T(8,128)(2,1)} %bitcast.72, ...), kind=kLoop, calls=%fused_computation.84 | loop fusion | bytes 33554496 | tf_op jit(solution)/shard_map/dynamic_slice | solution.py:63
  120.3 0.0 copy-start.16
  120.3 0.0 copy-done
  120.3 2.4 %fusion.23 = f32[8,512,256]{2,1,0:T(8,128)S(1)} fusion(bf16[8,512,1,128]{3,2,1,0:T(2,128)(2,1)} %get-tuple-element.17, bf16[8,512,256]{2,1,0:T(8,128)(2,1)S(1)} %copy-done), kind=kOutput, calls=%fused_computation.39 | convolution fusion | flops 268435456 | bytes 5767168 | tf_op jit(solution)/shard_map/prm,pmk->prk/dot_general | solution.py:65
  122.7 0.0 copy-start.19
  122.7 0.0 copy-start.20
  122.7 0.0 copy-start.15
  122.8 0.0 copy-done.16
  122.8 2.6 %fusion.24 = f32[8,512,256]{2,1,0:T(8,128)} fusion(bf16[8,512,1,128]{3,2,1,0:T(2,128)(2,1)S(1)} %copy-done.16, bf16[8,512,256]{2,1,0:T(8,128)(2,1)S(1)} %copy-done), kind=kOutput, calls=%fused_computation.41 | convolution fusion | flops 268435456 | bytes 6815744 | tf_op jit(solution)/shard_map/prm,pmk->prk/dot_general | solution.py:65
  125.4 0.0 collective-permute-done.2
  125.4 0.8 collective-permute-start.3
  126.2 0.0 copy-done.19
  126.2 0.0 copy-done.20
  126.3 0.1 divide_add_fusion
  126.3 0.0 copy-done.15
  126.3 2.7 %fusion.25 = f32[8,512,256]{2,1,0:T(8,128)} fusion(bf16[8,512,1,128]{3,2,1,0:T(2,128)(2,1)S(1)} %copy-done.15, bf16[8,512,256]{2,1,0:T(8,128)(2,1)S(1)} %copy-done), kind=kOutput, calls=%fused_computation.43 | convolution fusion | flops 268435456 | bytes 6815744 | tf_op jit(solution)/shard_map/prm,pmk->prk/dot_general | solution.py:65
  129.1 0.0 copy-done.14
  129.1 2.7 %fusion.26 = f32[8,512,256]{2,1,0:T(8,128)} fusion(bf16[8,512,1,128]{3,2,1,0:T(2,128)(2,1)S(1)} %copy-done.14, bf16[8,512,256]{2,1,0:T(8,128)(2,1)S(1)} %copy-done), kind=kOutput, calls=%fused_computation.45 | convolution fusion | flops 268435456 | bytes 6815744 | tf_op jit(solution)/shard_map/prm,pmk->prk/dot_general | solution.py:65
  131.8 0.0 collective-permute-done
  131.8 1.3 constant_dynamic-update-slice_fusion.1
  133.1 0.0 copy-start.13
  133.1 0.5 constant_dynamic-update-slice_fusion
  133.6 0.0 copy-start.17
  133.6 0.0 collective-permute-done.1
  133.6 0.1 constant_dynamic-update-slice_fusion.2
  133.7 0.0 copy-start.1
  133.7 0.0 copy-start.12
  133.7 1.1 copy-done.13
  134.8 5.3 %fusion.19 = f32[8,512,256]{2,1,0:T(8,128)} fusion(bf16[8,512,1,128]{3,2,1,0:T(2,128)(2,1)S(1)} %copy-done.13, bf16[8,512,256]{2,1,0:T(8,128)(2,1)} %collective-permute-done.2), kind=kOutput, calls=%fused_computation.31 | convolution fusion | flops 268435456 | bytes 5767168 | tf_op jit(solution)/shard_map/prm,pmk->prk/dot_general | solution.py:65
  140.2 0.0 copy-done.17
  140.2 0.0 copy-done.12
  140.2 3.8 %fusion.20 = f32[8,512,256]{2,1,0:T(8,128)} fusion(bf16[8,512,1,128]{3,2,1,0:T(2,128)(2,1)S(1)} %copy-done.12, bf16[8,512,256]{2,1,0:T(8,128)(2,1)} %collective-permute-done.2), kind=kOutput, calls=%fused_computation.33 | convolution fusion | flops 268435456 | bytes 5767168 | tf_op jit(solution)/shard_map/prm,pmk->prk/dot_general | solution.py:65
  144.0 0.0 copy-done.1
  144.0 5.5 %collective-permute-done.3 = bf16[8,512,256]{2,1,0:T(8,128)(2,1)S(1)} collective-permute-done((bf16[8,512,256]{2,1,0:T(8,128)(2,1)}, bf16[8,512,256]{2,1,0:T(8,128)(2,1)S(1)}, u32[]{:S(2)}, u32[]{:S(2)}) %collective-permute-start.3) | collective-permute-done | bytes 2097184 | tf_op jit(solution)/shard_map/ppermute | solution.py:26
  149.5 3.9 %collective-permute-start.4 = (bf16[8,512,256]{2,1,0:T(8,128)(2,1)S(1)}, bf16[8,512,256]{2,1,0:T(8,128)(2,1)S(1)}, u32[]{:S(2)}, u32[]{:S(2)}) collective-permute-start(bf16[8,512,256]{2,1,0:T(8,128)(2,1)S(1)} %collective-permute-done.3), channel_id=1, source_target_pairs={{3,0},{0,1},{1,2},{2,3},{7,4},{4,5},{5,6},{6,7},{11,8},{8,9},{9,10... | collective-permute-start | bytes 6291464 | tf_op jit(solution)/shard_map/ppermute | solution.py:26
  153.4 0.0 copy-done.11
  153.4 3.8 %fusion.21 = f32[8,512,256]{2,1,0:T(8,128)} fusion(bf16[8,512,1,128]{3,2,1,0:T(2,128)(2,1)S(1)} %copy-done.11, bf16[8,512,256]{2,1,0:T(8,128)(2,1)} %collective-permute-done.2), kind=kOutput, calls=%fused_computation.35 | convolution fusion | flops 268435456 | bytes 5767168 | tf_op jit(solution)/shard_map/prm,pmk->prk/dot_general | solution.py:65
  157.2 0.0 copy-done.10
  157.2 3.9 %fusion.22 = f32[8,512,256]{2,1,0:T(8,128)} fusion(bf16[8,512,1,128]{3,2,1,0:T(2,128)(2,1)S(1)} %copy-done.10, bf16[8,512,256]{2,1,0:T(8,128)(2,1)} %collective-permute-done.2), kind=kOutput, calls=%fused_computation.37 | convolution fusion | flops 268435456 | bytes 5767168 | tf_op jit(solution)/shard_map/prm,pmk->prk/dot_general | solution.py:65
  161.1 0.0 copy-done.9
  161.1 2.7 %fusion.15 = f32[8,512,256]{2,1,0:T(8,128)} fusion(bf16[8,512,1,128]{3,2,1,0:T(2,128)(2,1)S(1)} %copy-done.9, bf16[8,512,256]{2,1,0:T(8,128)(2,1)S(1)} %collective-permute-done.3), kind=kOutput, calls=%fused_computation.23 | convolution fusion | flops 268435456 | bytes 6815744 | tf_op jit(solution)/shard_map/prm,pmk->prk/dot_general | solution.py:65
  163.8 0.0 copy-done.8
  163.8 2.8 %fusion.16 = f32[8,512,256]{2,1,0:T(8,128)} fusion(bf16[8,512,1,128]{3,2,1,0:T(2,128)(2,1)S(1)} %copy-done.8, bf16[8,512,256]{2,1,0:T(8,128)(2,1)S(1)} %collective-permute-done.3), kind=kOutput, calls=%fused_computation.25 | convolution fusion | flops 268435456 | bytes 6815744 | tf_op jit(solution)/shard_map/prm,pmk->prk/dot_general | solution.py:65
  166.6 0.0 copy-done.7
  166.6 2.7 %fusion.17 = f32[8,512,256]{2,1,0:T(8,128)} fusion(bf16[8,512,1,128]{3,2,1,0:T(2,128)(2,1)S(1)} %copy-done.7, bf16[8,512,256]{2,1,0:T(8,128)(2,1)S(1)} %collective-permute-done.3), kind=kOutput, calls=%fused_computation.27 | convolution fusion | flops 268435456 | bytes 6815744 | tf_op jit(solution)/shard_map/prm,pmk->prk/dot_general | solution.py:65
  169.3 0.0 copy-done.6
  169.3 2.6 %fusion.18 = f32[8,512,256]{2,1,0:T(8,128)} fusion(bf16[8,512,1,128]{3,2,1,0:T(2,128)(2,1)S(1)} %copy-done.6, bf16[8,512,256]{2,1,0:T(8,128)(2,1)S(1)} %collective-permute-done.3), kind=kOutput, calls=%fused_computation.29 | convolution fusion | flops 268435456 | bytes 6815744 | tf_op jit(solution)/shard_map/prm,pmk->prk/dot_general | solution.py:65
  171.9 4.5 %collective-permute-done.4 = bf16[8,512,256]{2,1,0:T(8,128)(2,1)S(1)} collective-permute-done((bf16[8,512,256]{2,1,0:T(8,128)(2,1)S(1)}, bf16[8,512,256]{2,1,0:T(8,128)(2,1)S(1)}, u32[]{:S(2)}, u32[]{:S(2)}) %collective-permute-start.4) | collective-permute-done | bytes 2097184 | tf_op jit(solution)/shard_map/ppermute | solution.py:26
  176.4 0.0 copy-done.5
  176.4 2.7 %fusion.12 = f32[8,512,256]{2,1,0:T(8,128)} fusion(bf16[8,512,1,128]{3,2,1,0:T(2,128)(2,1)S(1)} %copy-done.5, bf16[8,512,256]{2,1,0:T(8,128)(2,1)S(1)} %collective-permute-done.4), kind=kOutput, calls=%fused_computation.17 | convolution fusion | flops 268435456 | bytes 6815744 | tf_op jit(solution)/shard_map/prm,pmk->prk/dot_general | solution.py:65
  179.1 0.0 copy-done.4
  179.1 2.8 %fusion.13 = f32[8,512,256]{2,1,0:T(8,128)} fusion(bf16[8,512,1,128]{3,2,1,0:T(2,128)(2,1)S(1)} %copy-done.4, bf16[8,512,256]{2,1,0:T(8,128)(2,1)S(1)} %collective-permute-done.4), kind=kOutput, calls=%fused_computation.19 | convolution fusion | flops 268435456 | bytes 6815744 | tf_op jit(solution)/shard_map/prm,pmk->prk/dot_general | solution.py:65
  181.8 0.0 copy-done.18
  181.8 2.7 %fusion.14 = f32[8,512,256]{2,1,0:T(8,128)} fusion(bf16[8,512,1,128]{3,2,1,0:T(2,128)(2,1)S(1)} %copy-done.3, bf16[8,512,256]{2,1,0:T(8,128)(2,1)S(1)} %collective-permute-done.4), kind=kOutput, calls=%fused_computation.21 | convolution fusion | flops 268435456 | bytes 6815744 | tf_op jit(solution)/shard_map/prm,pmk->prk/dot_general | solution.py:65
  184.5 27.1 %fusion.10 = bf16[8,512,256]{2,1,0:T(8,128)(2,1)} fusion(bf16[8,512,256]{2,1,0:T(8,128)(2,1)} %param.8, f32[8,512,256]{2,1,0:T(8,128)} %fusion.12, f32[8,512,256]{2,1,0:T(8,128)} %fusion.14, f32[8,512,256]{2,1,0:T(8,128)} %fusion.13, f32[8,512,256]{2,1,0:T(8,128)} %fusion.15, f32[8,512,256]{2,1,0:T(8,128)} %fusion.16, f32[8,512,256]{2,1,0:T(8,128)} %fusion.18, ...), kind=kOutput, calls=%fused_computation.13 | convolution fusion | flops 320864256 | bytes 87572480 | tf_op jit(solution)/shard_map/prm,pmk->prk/dot_general | solution.py:65
  (16 shorter events, 0.0 us)
Async XLA Ops:
  0.0 14.9 %copy-start.21 = (s32[16]{0:T(128)S(1)}, s32[16]{0:T(128)}, u32[]{:S(2)}) copy-start(s32[16]{0:T(128)} %param.12) | copy-start | bytes 196
  0.0 125.4 %collective-permute-start.2 = (bf16[8,512,256]{2,1,0:T(8,128)(2,1)}, bf16[8,512,256]{2,1,0:T(8,128)(2,1)}, u32[]{:S(2)}, u32[]{:S(2)}) collective-permute-start(bf16[8,512,256]{2,1,0:T(8,128)(2,1)} %param.7), channel_id=1, source_target_pairs={{3,0},{0,1},{1,2},{2,3},{7,4},{4,5},{5,6},{6,7},{11,8},{8,9},{9,10... | collective-permute-start | bytes 6291464 | tf_op jit(solution)/shard_map/ppermute | solution.py:26
  6.5 125.3 %collective-permute-start = (bf16[4,512,256]{2,1,0:T(8,128)(2,1)}, bf16[4,512,256]{2,1,0:T(8,128)(2,1)}, u32[]{:S(2)}, u32[]{:S(2)}) collective-permute-start(bf16[4,512,256]{2,1,0:T(8,128)(2,1)} %get-tuple-element.23), channel_id=1, source_target_pairs={{0,4},{4,8},{8,12},{12,16},{16,20},{20,24},{24,28},{28,32},{32,36}... | collective-permute-start | bytes 3145736 | tf_op jit(solution)/shard_map/ppermute | solution.py:37
  9.6 124.0 %collective-permute-start.1 = (bf16[4,512,256]{2,1,0:T(8,128)(2,1)}, bf16[4,512,256]{2,1,0:T(8,128)(2,1)S(1)}, u32[]{:S(2)}, u32[]{:S(2)}) collective-permute-start(bf16[4,512,256]{2,1,0:T(8,128)(2,1)} %get-tuple-element.24), channel_id=1, source_target_pairs={{4,0},{8,4},{12,8},{16,12},{20,16},{24,20},{28,24},{32,28},{36,32}... | collective-permute-start | bytes 3145736 | tf_op jit(solution)/shard_map/ppermute | solution.py:39
  61.7 58.6 %copy-start = (bf16[8,512,256]{2,1,0:T(8,128)(2,1)S(1)}, bf16[8,512,256]{2,1,0:T(8,128)(2,1)}, u32[]{:S(2)}) copy-start(bf16[8,512,256]{2,1,0:T(8,128)(2,1)} %param.7) | copy-start | bytes 6291460
  120.3 2.5 %copy-start.16 = (bf16[8,512,1,128]{3,2,1,0:T(2,128)(2,1)S(1)}, bf16[8,512,1,128]{3,2,1,0:T(2,128)(2,1)}, u32[]{:S(2)}) copy-start(bf16[8,512,1,128]{3,2,1,0:T(2,128)(2,1)} %get-tuple-element.18) | copy-start | bytes 3145732
  122.7 3.5 %copy-start.19 = (f32[512]{0:T(512)S(1)}, f32[512]{0:T(512)}, u32[]{:S(2)}) copy-start(f32[512]{0:T(512)} %param.11) | copy-start | bytes 6148
  122.7 3.5 %copy-start.20 = (f32[512]{0:T(512)S(1)}, f32[512]{0:T(512)}, u32[]{:S(2)}) copy-start(f32[512]{0:T(512)} %param.10) | copy-start | bytes 6148
  122.7 3.6 %copy-start.15 = (bf16[8,512,1,128]{3,2,1,0:T(2,128)(2,1)S(1)}, bf16[8,512,1,128]{3,2,1,0:T(2,128)(2,1)}, u32[]{:S(2)}) copy-start(bf16[8,512,1,128]{3,2,1,0:T(2,128)(2,1)} %get-tuple-element.19) | copy-start | bytes 3145732
  125.4 3.7 %copy-start.14 = (bf16[8,512,1,128]{3,2,1,0:T(2,128)(2,1)S(1)}, bf16[8,512,1,128]{3,2,1,0:T(2,128)(2,1)}, u32[]{:S(2)}) copy-start(bf16[8,512,1,128]{3,2,1,0:T(2,128)(2,1)} %get-tuple-element.20) | copy-start | bytes 3145732
  125.4 24.1 %collective-permute-start.3 = (bf16[8,512,256]{2,1,0:T(8,128)(2,1)}, bf16[8,512,256]{2,1,0:T(8,128)(2,1)S(1)}, u32[]{:S(2)}, u32[]{:S(2)}) collective-permute-start(bf16[8,512,256]{2,1,0:T(8,128)(2,1)} %collective-permute-done.2), channel_id=1, source_target_pairs={{3,0},{0,1},{1,2},{2,3},{7,4},{4,5},{5,6},{6,7},{11,8},{8,9},{9,10... | collective-permute-start | bytes 6291464 | tf_op jit(solution)/shard_map/ppermute | solution.py:26
  133.1 1.8 copy-start.13
  133.6 6.6 %copy-start.17 = (bf16[12,512,256]{2,1,0:T(8,128)(2,1)}, bf16[12,512,256]{2,1,0:T(8,128)(2,1)S(1)}, u32[]{:S(2)}) copy-start(bf16[12,512,256]{2,1,0:T(8,128)(2,1)S(1)} %get-tuple-element.21) | copy-start | bytes 9437188
  133.7 10.3 %copy-start.1 = (bf16[12,512,256]{2,1,0:T(8,128)(2,1)}, bf16[12,512,256]{2,1,0:T(8,128)(2,1)S(1)}, u32[]{:S(2)}) copy-start(bf16[12,512,256]{2,1,0:T(8,128)(2,1)S(1)} %constant_dynamic-update-slice_fusion.2) | copy-start | bytes 9437188
  133.7 6.5 %copy-start.12 = (bf16[8,512,1,128]{3,2,1,0:T(2,128)(2,1)S(1)}, bf16[8,512,1,128]{3,2,1,0:T(2,128)(2,1)}, u32[]{:S(2)}) copy-start(bf16[8,512,1,128]{3,2,1,0:T(2,128)(2,1)} %get-tuple-element.14) | copy-start | bytes 3145732
  140.2 13.3 %copy-start.11 = (bf16[8,512,1,128]{3,2,1,0:T(2,128)(2,1)S(1)}, bf16[8,512,1,128]{3,2,1,0:T(2,128)(2,1)}, u32[]{:S(2)}) copy-start(bf16[8,512,1,128]{3,2,1,0:T(2,128)(2,1)} %get-tuple-element.15) | copy-start | bytes 3145732
  144.0 13.2 %copy-start.10 = (bf16[8,512,1,128]{3,2,1,0:T(2,128)(2,1)S(1)}, bf16[8,512,1,128]{3,2,1,0:T(2,128)(2,1)}, u32[]{:S(2)}) copy-start(bf16[8,512,1,128]{3,2,1,0:T(2,128)(2,1)} %get-tuple-element.16) | copy-start | bytes 3145732
  149.5 26.9 %collective-permute-start.4 = (bf16[8,512,256]{2,1,0:T(8,128)(2,1)S(1)}, bf16[8,512,256]{2,1,0:T(8,128)(2,1)S(1)}, u32[]{:S(2)}, u32[]{:S(2)}) collective-permute-start(bf16[8,512,256]{2,1,0:T(8,128)(2,1)S(1)} %collective-permute-done.3), channel_id=1, source_target_pairs={{3,0},{0,1},{1,2},{2,3},{7,4},{4,5},{5,6},{6,7},{11,8},{8,9},{9,10... | collective-permute-start | bytes 6291464 | tf_op jit(solution)/shard_map/ppermute | solution.py:26
  157.2 3.9 %copy-start.9 = (bf16[8,512,1,128]{3,2,1,0:T(2,128)(2,1)S(1)}, bf16[8,512,1,128]{3,2,1,0:T(2,128)(2,1)}, u32[]{:S(2)}) copy-start(bf16[8,512,1,128]{3,2,1,0:T(2,128)(2,1)} %get-tuple-element.9) | copy-start | bytes 3145732
  161.1 2.7 %copy-start.8 = (bf16[8,512,1,128]{3,2,1,0:T(2,128)(2,1)S(1)}, bf16[8,512,1,128]{3,2,1,0:T(2,128)(2,1)}, u32[]{:S(2)}) copy-start(bf16[8,512,1,128]{3,2,1,0:T(2,128)(2,1)} %get-tuple-element.10) | copy-start | bytes 3145732
  163.8 2.8 %copy-start.7 = (bf16[8,512,1,128]{3,2,1,0:T(2,128)(2,1)S(1)}, bf16[8,512,1,128]{3,2,1,0:T(2,128)(2,1)}, u32[]{:S(2)}) copy-start(bf16[8,512,1,128]{3,2,1,0:T(2,128)(2,1)} %get-tuple-element.11) | copy-start | bytes 3145732
  166.6 2.7 %copy-start.6 = (bf16[8,512,1,128]{3,2,1,0:T(2,128)(2,1)S(1)}, bf16[8,512,1,128]{3,2,1,0:T(2,128)(2,1)}, u32[]{:S(2)}) copy-start(bf16[8,512,1,128]{3,2,1,0:T(2,128)(2,1)} %get-tuple-element.12) | copy-start | bytes 3145732
  169.3 7.1 %copy-start.5 = (bf16[8,512,1,128]{3,2,1,0:T(2,128)(2,1)S(1)}, bf16[8,512,1,128]{3,2,1,0:T(2,128)(2,1)}, u32[]{:S(2)}) copy-start(bf16[8,512,1,128]{3,2,1,0:T(2,128)(2,1)} %get-tuple-element.6) | copy-start | bytes 3145732
  171.9 7.2 %copy-start.4 = (bf16[8,512,1,128]{3,2,1,0:T(2,128)(2,1)S(1)}, bf16[8,512,1,128]{3,2,1,0:T(2,128)(2,1)}, u32[]{:S(2)}) copy-start(bf16[8,512,1,128]{3,2,1,0:T(2,128)(2,1)} %get-tuple-element.7) | copy-start | bytes 3145732
  176.4 5.4 %copy-start.18 = (bf16[8,512,256]{2,1,0:T(8,128)(2,1)}, bf16[8,512,256]{2,1,0:T(8,128)(2,1)S(1)}, u32[]{:S(2)}) copy-start(bf16[8,512,256]{2,1,0:T(8,128)(2,1)S(1)} %collective-permute-done.4) | copy-start | bytes 6291460
  179.1 2.8 %copy-start.3 = (bf16[8,512,1,128]{3,2,1,0:T(2,128)(2,1)S(1)}, bf16[8,512,1,128]{3,2,1,0:T(2,128)(2,1)}, u32[]{:S(2)}) copy-start(bf16[8,512,1,128]{3,2,1,0:T(2,128)(2,1)} %get-tuple-element.8) | copy-start | bytes 3145732
  181.8 2.7 %copy-start.2 = (bf16[8,512,1,128]{3,2,1,0:T(2,128)(2,1)S(1)}, bf16[8,512,1,128]{3,2,1,0:T(2,128)(2,1)}, u32[]{:S(2)}) copy-start(bf16[8,512,1,128]{3,2,1,0:T(2,128)(2,1)} %get-tuple-element.5) | copy-start | bytes 3145732
where the time goes:
time: 213 us; the launch traced here: 212 us
  local copies, waits for them, and re-layouts  79.9 us (38%)
  matrix products  73.3 us (34%)
  between operations  32 us (15%)
  starting transfers between devices  16.5 us (8%)
  waiting for transfers between devices  10 us (5%)
    dot_general x16, matrix products, product_part(): jnp.einsum('prm,pmk->prk', matrices, vectors, preferred_element_type=jnp....  73.3 us
    dynamic_slice x1, local copies, waits for them, and re-layouts, product_part(): matrices = lax.dynamic_slice_in_dim(blocked, column_block, 1, 2)[:, :, 0, :]  57.9 us
    unnamed x46, local copies, waits for them, and re-layouts  17.6 us
    ppermute x3, waiting for transfers between devices, from_behind(): return lax.ppermute(block, axis, route)  10 us
    ppermute x3, starting transfers between devices, from_behind(): return lax.ppermute(block, axis, route)  8.17 us
    ppermute x1, starting transfers between devices, padded_2(): lax.ppermute(head, axis, [((i + 1) % count, i) for i in range(ends)])  5.17 us
  transfers between devices with their start and end apart: 5, of which 2 were waited for; matrix products, arithmetic and copies ran while one was open for 55% of the time, Pallas kernels for 0%

commit v1 on v0

v1 whole, which is shorter than its diff:
```python
import functools

import jax
import jax.numpy as jnp
from jax import lax
from jax.experimental import pallas as pl
from jax.experimental.pallas import tpu as pltpu
from jax.sharding import PartitionSpec as P

CHB = 128
GRID = 8192
MESH = pl.DeviceIdType.MESH
TAPS = (-205.0 / 72, 8.0 / 5, -1.0 / 5, 8.0 / 315, -1.0 / 560)
LANES = 128
TILE = 16


def kernel(
    amp, prev, coup, thr, bar, order, offset, out,
    cbuf, vecs, relay_t, relay_a, halo_lo, halo_hi, pbuf, acc, thr_b, bar_b, scale, columns,
    coup_sem, own_sem, prev_sem, out_sem,
    t_send, t_recv, a_send, a_recv, ft_send, fa_send, far_recv,
    sib_send, sib_recv, fs_send, fs_recv, up_send, up_recv, down_send, down_recv,
):
    points, rows, width = amp.shape
    half = points // 2
    per = rows // CHB
    radial, chan = lax.axis_index("radial"), lax.axis_index("chan")
    x, yl, z = radial % 4, (radial // 4) % 2, radial // 8
    yh, core = chan // 2, chan % 2
    last = 3

    def at(px, pyl, pz, pyh, pcore):
        return ((pz * 2 + pyl) * 4 + px, pyh * 2 + pcore)

    toward = at(x, 1 - yl, z, yh, core)
    away = at(x, 1 - yl, z, 1 - yh, core)
    sibling = at(x, yl, z, yh, 1 - core)
    up_z = jnp.where(x == last, z + (1 - yl), z)
    up_to = at((x + 1) % 4, yl, jnp.minimum(up_z, 3), yh, core)
    has_up_to = up_z <= 3
    down_z = jnp.where(x == 0, z - yl, z)
    down_to = at((x + 3) % 4, yl, jnp.maximum(down_z, 0), yh, core)
    has_down_to = down_z >= 0
    up_fz = jnp.where(x == 0, z - (1 - yl), z)
    up_from = at((x + 3) % 4, yl, jnp.maximum(up_fz, 0), yh, core)
    has_up_from = up_fz >= 0
    down_fz = jnp.where(x == last, z + yl, z)
    down_from = at((x + 1) % 4, yl, jnp.minimum(down_fz, 3), yh, core)
    has_down_from = down_fz <= 3
    t_base = jnp.where(x < 2, 0, half)
    a_base = half - t_base

    def remote(src, dst, send, recv, to):
        return pltpu.make_async_remote_copy(
            src_ref=src, dst_ref=dst, send_sem=send, recv_sem=recv, device_id=to, device_id_type=MESH
        )

    def own_t(i):
        return remote(amp.at[t_base + i], relay_t.at[i], t_send.at[i], t_recv.at[i], toward)

    def own_a(i):
        return remote(amp.at[a_base + i], relay_a.at[i], a_send.at[i], a_recv.at[i], away)

    def fwd_t(i):
        p = t_base + i
        return remote(relay_t.at[i], vecs.at[2, p], ft_send.at[i], far_recv.at[p], away)

    def fwd_a(i):
        p = a_base + i
        return remote(relay_a.at[i], vecs.at[2, p], fa_send.at[i], far_recv.at[p], toward)

    def own_sib(p):
        return remote(amp.at[p], vecs.at[1, p], sib_send.at[p], sib_recv.at[p], sibling)

    def fwd_sib(p):
        return remote(vecs.at[2, p], vecs.at[3, p], fs_send.at[p], fs_recv.at[p], sibling)

    def up_own(i):
        return remote(amp.at[half + i], halo_lo.at[i], up_send.at[i], up_recv.at[i], up_to)

    def up_relay(i):
        return remote(relay_t.at[i], halo_lo.at[i], up_send.at[i], up_recv.at[i], up_to)

    def down_own(i):
        return remote(amp.at[i], halo_hi.at[i], down_send.at[i], down_recv.at[i], down_to)

    def down_relay(i):
        return remote(relay_t.at[i], halo_hi.at[i], down_send.at[i], down_recv.at[i], down_to)

    blocks = coup.shape[2] // CHB

    def coup_copy(p, b):
        part = coup.at[p, :, b * CHB : (b + 1) * CHB]
        return pltpu.make_async_copy(part, cbuf.at[p, b], coup_sem.at[p, b])

    def coup_all(step):
        def one(p, _):
            for b in range(blocks):
                step(coup_copy(p, b))
            return 0

        lax.fori_loop(0, points, one, 0)

    own_copy = pltpu.make_async_copy(amp, vecs.at[0], own_sem)
    prev_copy = pltpu.make_async_copy(prev, pbuf, prev_sem)

    def out_copy(p):
        return pltpu.make_async_copy(pbuf.at[p], out.at[p], out_sem.at[p])

    barrier = pltpu.get_barrier_semaphore()
    for to in (toward, away, sibling):
        pl.semaphore_signal(barrier, inc=1, device_id=to, device_id_type=MESH)

    @pl.when(has_up_from)
    def _():
        pl.semaphore_signal(barrier, inc=1, device_id=up_from, device_id_type=MESH)

    @pl.when(has_down_from)
    def _():
        pl.semaphore_signal(barrier, inc=1, device_id=down_from, device_id_type=MESH)

    own_copy.start()
    pl.semaphore_wait(
        barrier, 3 + jnp.where(has_up_to, 1, 0) + jnp.where(has_down_to, 1, 0)
    )
    for i in range(half):
        own_t(i).start()
        own_a(i).start()
    for p in range(points):
        own_sib(p).start()
    for i in range(half):
        @pl.when(x < last)
        def _(i=i):
            up_own(i).start()

        @pl.when(x > 0)
        def _(i=i):
            down_own(i).start()
    coup_all(lambda c: c.start())
    prev_copy.start()

    @pl.when(jnp.logical_not(has_up_from))
    def _():
        halo_lo[...] = jnp.zeros_like(halo_lo)

    @pl.when(jnp.logical_not(has_down_from))
    def _():
        halo_hi[...] = jnp.zeros_like(halo_hi)

    for j in range(per):
        part = slice(j * CHB, (j + 1) * CHB)
        thr_b[part, :] = jnp.broadcast_to(thr[part].reshape(1, CHB), (CHB, LANES)).T
        bar_b[part, :] = jnp.broadcast_to(bar[part].reshape(1, CHB), (CHB, LANES)).T
    for p in range(points):
        place = jnp.full((TILE, LANES), offset[0] + radial * points + p + 1, jnp.int32)
        s = place.astype(jnp.float32) * (1.0 / (GRID // 16))
        scale[p] = 1.0 / (1.0 + s * s)

    own_copy.wait()
    coup_all(lambda c: c.wait())

    sources = (chan, yh * 2 + 1 - core, (1 - yh) * 2 + core, (1 - yh) * 2 + 1 - core)

    def column(j):
        found = jnp.int32(0)
        for b in range(order.shape[0]):
            found = found + b * (1 - jnp.minimum((order[b] - j) * (order[b] - j), 1))
        return jnp.minimum(found, order.shape[0] - 1)

    for k, s in enumerate(sources):
        for j in range(per):
            columns[k * per + j] = column(s * per + j)

    def product(p, which):
        lhs = jnp.concatenate(
            [
                cbuf[p, columns[s * per + j]]
                for s in which
                for j in range(per)
            ],
            axis=1,
        )
        rhs = jnp.concatenate([vecs[s, p] for s in which], axis=0)
        return jnp.dot(lhs, rhs, preferred_element_type=jnp.float32)

    def first_hop(i, _):
        t = own_t(i)
        t.wait_recv()
        fwd_t(i).start()

        @pl.when(jnp.logical_and(x == last, has_up_to))
        def _():
            up_relay(i).start()

        @pl.when(jnp.logical_and(x == 0, has_down_to))
        def _():
            down_relay(i).start()

        own_a(i).wait_recv()
        fwd_a(i).start()

        def local(q, _):
            p = i * 2 + q
            own_sib(p).wait_recv()
            acc[p] = product(p, (0, 1))
            return 0

        lax.fori_loop(0, 2, local, 0)
        return 0

    lax.fori_loop(0, half, first_hop, 0)

    def arrive(i):
        for p in (t_base + i, a_base + i):
            remote(vecs.at[2, p], vecs.at[2, p], ft_send.at[i], far_recv.at[p], away).wait_recv()
            fwd_sib(p).start()

    def finish(i, write):
        def one(q, _):
            p = i + q * half
            fwd_sib(p).wait_recv()
            if write:
                pbuf[p] = ((acc[p] + product(p, (2, 3))) * (1.0 / 3.0)).astype(pbuf.dtype)
                out_copy(p).start()
            else:
                acc[p] += product(p, (2, 3))
            return 0

        lax.fori_loop(0, 2, one, 0)

    def store(i):
        for p in (i, i + half):
            pbuf[p] = (acc[p] * (1.0 / 3.0)).astype(pbuf.dtype)
            out_copy(p).start()

    arrive(0)
    finish(0, False)
    arrive(1)
    finish(1, False)

    @pl.when(has_up_from)
    def _():
        for i in range(half):
            up_own(i).wait_recv()

    @pl.when(has_down_from)
    def _():
        for i in range(half):
            down_own(i).wait_recv()

    prev_copy.wait()

    def stencil(r, _):
        tile = pl.ds(pl.multiple_of(r * TILE, TILE), TILE)
        for l in range(width // LANES):
            lane = slice(l * LANES, (l + 1) * LANES)
            v = [halo_lo[i, tile, lane].astype(jnp.float32) for i in range(half)]
            v += [vecs[0, i, tile, lane].astype(jnp.float32) for i in range(points)]
            v += [halo_hi[i, tile, lane].astype(jnp.float32) for i in range(half)]
            base = thr_b[tile, :] - (1.0 + 0.5 * TAPS[0])
            slope = bar_b[tile, :]
            for p in range(points):
                c = p + half
                total = (base + slope * scale[p]) * v[c]
                for m in range(1, 5):
                    total = total + (-0.5 * TAPS[m]) * (v[c - m] + v[c + m])
                total = total - 3.0 * pbuf[p, tile, lane].astype(jnp.float32)
                acc[p, tile, lane] = acc[p, tile, lane] + total
        return 0

    lax.fori_loop(0, rows // TILE, stencil, 0)
    store(0)
    store(1)
    arrive(2)
    finish(2, True)
    arrive(3)
    finish(3, True)

    for i in range(half):
        own_t(i).wait_send()
        own_a(i).wait_send()
        fwd_t(i).wait_send()
        fwd_a(i).wait_send()
    for p in range(points):
        own_sib(p).wait_send()
        fwd_sib(p).wait_send()

    @pl.when(has_up_to)
    def _():
        for i in range(half):
            up_relay(i).wait_send()

    @pl.when(has_down_to)
    def _():
        for i in range(half):
            down_relay(i).wait_send()

    for p in range(points):
        out_copy(p).wait()


def local(amplitudes, previous, coupling, thresholds, barrier, block_order, window_offset):
    points, rows, width = amplitudes.shape
    half = points // 2
    columns = coupling.shape[2]
    bf16, f32 = jnp.bfloat16, jnp.float32
    sem = pltpu.SemaphoreType.DMA
    any_spec = pl.BlockSpec(memory_space=pl.ANY)
    vmem_spec = pl.BlockSpec(memory_space=pltpu.VMEM)
    smem_spec = pl.BlockSpec(memory_space=pltpu.SMEM)
    return pl.pallas_call(
        kernel,
        out_shape=jax.ShapeDtypeStruct((points, rows, width), bf16),
        in_specs=[any_spec] * 3 + [vmem_spec] * 2 + [smem_spec] * 2,
        out_specs=any_spec,
        scratch_shapes=[
            pltpu.VMEM((points, columns // CHB, rows, CHB), bf16),
            pltpu.VMEM((4, points, rows, width), bf16),
            pltpu.VMEM((half, rows, width), bf16),
            pltpu.VMEM((half, rows, width), bf16),
            pltpu.VMEM((half, rows, width), bf16),
            pltpu.VMEM((half, rows, width), bf16),
            pltpu.VMEM((points, rows, width), bf16),
            pltpu.VMEM((points, rows, width), f32),
            pltpu.VMEM((rows, LANES), f32),
            pltpu.VMEM((rows, LANES), f32),
            pltpu.VMEM((points, TILE, LANES), f32),
            pltpu.SMEM((columns // CHB,), jnp.int32),
            sem((points, columns // CHB)), sem, sem, sem((points,)),
            sem((half,)), sem((half,)), sem((half,)), sem((half,)),
            sem((half,)), sem((half,)), sem((points,)),
            sem((points,)), sem((points,)), sem((points,)), sem((points,)),
            sem((half,)), sem((half,)), sem((half,)), sem((half,)),
        ],
        compiler_params=pltpu.CompilerParams(
            collective_id=0, has_side_effects=True, vmem_limit_bytes=60 << 20
        ),
        cost_estimate=pl.CostEstimate(
            flops=2 * points * rows * columns * width,
            bytes_accessed=2 * points * rows * (columns + 3 * width),
            transcendentals=0,
        ),
    )(amplitudes, previous, coupling, thresholds, barrier, block_order, window_offset)


def solution(mesh):
    placed = (
        P("radial", "chan", None),
        P("radial", "chan", None),
        P("radial", "chan", None),
        P("chan"),
        P("chan"),
        P(),
        P(),
    )
    return jax.shard_map(
        local, mesh=mesh, in_specs=placed, out_specs=P("radial", "chan", None), check_vma=False
    )
```

time: 213 us -> 61.2 us (0.29)
  local copies, waits for them, and re-layouts: 79.9 us -> 3.05 us
  matrix products: 73.3 us -> 0 us
  Pallas kernels: 0 us -> 57.4 us
  between operations: 32 us -> 0.66 us
  starting transfers between devices: 16.5 us -> 0 us
  waiting for transfers between devices: 10 us -> 0 us
    dot_general x16 -> x0, matrix products: 73.3 us -> none  [product_part(): jnp.einsum('prm,pmk->prk', matrices, vectors, preferred_element_type=jnp....]
    dynamic_slice x2 -> x0, local copies, waits for them, and re-layouts: 58.7 us -> none  [the longest x1 57.9 us: product_part(): matrices = lax.dynamic_slice_in_dim(blocked, column_block, 1, 2)[:, :, 0, :]]
    pallas_call x0 -> x1, Pallas kernels: none -> 57.4 us  [local(): pl.pallas_call(kernel, out_shape=jax.ShapeDtypeStruct((points, rows, widt...]
    ppermute x5 -> x0, starting transfers between devices: 16.5 us -> none  [the longest x3 8.17 us: from_behind(): return lax.ppermute(block, axis, route)]
    unnamed x46 -> x1, local copies, waits for them, and re-layouts: 17.6 us -> 3.05 us
    ppermute x5 -> x0, waiting for transfers between devices: 10 us -> none  [the longest x3 10 us: from_behind(): return lax.ppermute(block, axis, route)]
    slice x1 -> x0, local copies, waits for them, and re-layouts: 2.98 us -> none  [padded_2(): lax.slice_in_dim(cells, cells.shape[dim] - width, cells.shape[dim], axis=...]
  transfers between devices with their start and end apart: 5 -> 0, of which waited for: 2 -> 0; matrix products, arithmetic and copies ran while one was open for 55% -> 0% of each run, Pallas kernels for 0% -> 0%
where the time goes in v1:
time: 61.2 us; the launch traced here: 61.1 us
  Pallas kernels  57.4 us (94%)
  local copies, waits for them, and re-layouts  3.05 us (5%)
  between operations  0.66 us (1%)
    pallas_call x1, Pallas kernels, local(): pl.pallas_call(kernel, out_shape=jax.ShapeDtypeStruct((points, rows, widt...  57.4 us
    unnamed x1, local copies, waits for them, and re-layouts  3.05 us

profile of v1, /device:TPU:97, one launch (start us, length us, event | category | flops | bytes accessed | tf_op | source)
XLA Modules:
  0.0 61.1 jit_solution(15657112729569189394)
XLA Ops:
  0.7 57.4 %shard_map.73 = bf16[8,512,256]{2,1,0:T(8,128)(2,1)} custom-call(bf16[8,512,256]{2,1,0:T(8,128)(2,1)} %amp.1, bf16[8,512,256]{2,1,0:T(8,128)(2,1)} %prev.1, bf16[8,512,2048]{2,1,0:T(8,128)(2,1)} %coup.1, f32[512]{0:T(512)} %thr.1, f32[512]{0:T(512)} %bar.1, s32[16]{0:T(128)} %order.1, s32[1]{0:T(128)S(6)} %copy.9.offset), custom_call_target="tpu_custom_call" | custom-call | flops 4294967296 | bytes 23068672 | tf_op jit(solution)/shard_map/pallas_call | solution.py:312
  58.0 3.0 %copy.10 = bf16[8,512,256]{2,1,0:T(8,128)(2,1)} copy(bf16[8,512,256]{2,1,0:T(8,128)(2,1)} %shard_map.73) | data formatting | bytes 4194304

commit v2 on v1

--- a/solution.py
+++ b/solution.py
@@ -16,9 +16,10 @@
 
 
 def kernel(
-    amp, prev, coup, thr, bar, order, offset, out,
+    amp, prev, coup, thr_in, bar_in, order_in, offset_in, out,
     cbuf, vecs, relay_t, relay_a, halo_lo, halo_hi, pbuf, acc, thr_b, bar_b, scale, columns,
-    coup_sem, own_sem, prev_sem, out_sem,
+    thr, bar, order, offset, small_sem,
+    coup_sem, own_sem, prev_sem,
     t_send, t_recv, a_send, a_recv, ft_send, fa_send, far_recv,
     sib_send, sib_recv, fs_send, fs_recv, up_send, up_recv, down_send, down_recv,
 ):
@@ -102,11 +103,14 @@
 
         lax.fori_loop(0, points, one, 0)
 
+    small = [
+        pltpu.make_async_copy(a, b, small_sem.at[i])
+        for i, (a, b) in enumerate(
+            ((thr_in, thr), (bar_in, bar), (order_in, order), (offset_in, offset))
+        )
+    ]
     own_copy = pltpu.make_async_copy(amp, vecs.at[0], own_sem)
     prev_copy = pltpu.make_async_copy(prev, pbuf, prev_sem)
-
-    def out_copy(p):
-        return pltpu.make_async_copy(pbuf.at[p], out.at[p], out_sem.at[p])
 
     barrier = pltpu.get_barrier_semaphore()
     for to in (toward, away, sibling):
@@ -121,6 +125,8 @@
         pl.semaphore_signal(barrier, inc=1, device_id=down_from, device_id_type=MESH)
 
     own_copy.start()
+    for copy in small:
+        copy.start()
     pl.semaphore_wait(
         barrier, 3 + jnp.where(has_up_to, 1, 0) + jnp.where(has_down_to, 1, 0)
     )
@@ -148,6 +154,8 @@
     def _():
         halo_hi[...] = jnp.zeros_like(halo_hi)
 
+    for copy in small:
+        copy.wait()
     for j in range(per):
         part = slice(j * CHB, (j + 1) * CHB)
         thr_b[part, :] = jnp.broadcast_to(thr[part].reshape(1, CHB), (CHB, LANES)).T
@@ -221,8 +229,7 @@
             p = i + q * half
             fwd_sib(p).wait_recv()
             if write:
-                pbuf[p] = ((acc[p] + product(p, (2, 3))) * (1.0 / 3.0)).astype(pbuf.dtype)
-                out_copy(p).start()
+                out[p] = ((acc[p] + product(p, (2, 3))) * (1.0 / 3.0)).astype(out.dtype)
             else:
                 acc[p] += product(p, (2, 3))
             return 0
@@ -231,8 +238,7 @@
 
     def store(i):
         for p in (i, i + half):
-            pbuf[p] = (acc[p] * (1.0 / 3.0)).astype(pbuf.dtype)
-            out_copy(p).start()
+            out[p] = (acc[p] * (1.0 / 3.0)).astype(out.dtype)
 
     arrive(0)
     finish(0, False)
@@ -296,8 +302,16 @@
         for i in range(half):
             down_relay(i).wait_send()
 
-    for p in range(points):
-        out_copy(p).wait()
+
+def write_out(staged, out, sems):
+    copies = [
+        pltpu.make_async_copy(staged.at[p], out.at[p], sems.at[p])
+        for p in range(staged.shape[0])
+    ]
+    for copy in copies:
+        copy.start()
+    for copy in copies:
+        copy.wait()
 
 
 def local(amplitudes, previous, coupling, thresholds, barrier, block_order, window_offset):
@@ -308,12 +322,11 @@
     sem = pltpu.SemaphoreType.DMA
     any_spec = pl.BlockSpec(memory_space=pl.ANY)
     vmem_spec = pl.BlockSpec(memory_space=pltpu.VMEM)
-    smem_spec = pl.BlockSpec(memory_space=pltpu.SMEM)
-    return pl.pallas_call(
+    staged = pl.pallas_call(
         kernel,
-        out_shape=jax.ShapeDtypeStruct((points, rows, width), bf16),
-        in_specs=[any_spec] * 3 + [vmem_spec] * 2 + [smem_spec] * 2,
-        out_specs=any_spec,
+        out_shape=pltpu.VMEM((points, rows, width), bf16),
+        in_specs=[any_spec] * 7,
+        out_specs=vmem_spec,
         scratch_shapes=[
             pltpu.VMEM((points, columns // CHB, rows, CHB), bf16),
             pltpu.VMEM((4, points, rows, width), bf16),
@@ -327,7 +340,12 @@
             pltpu.VMEM((rows, LANES), f32),
             pltpu.VMEM((points, TILE, LANES), f32),
             pltpu.SMEM((columns // CHB,), jnp.int32),
-            sem((points, columns // CHB)), sem, sem, sem((points,)),
+            pltpu.VMEM(thresholds.shape, f32),
+            pltpu.VMEM(barrier.shape, f32),
+            pltpu.SMEM(block_order.shape, jnp.int32),
+            pltpu.SMEM(window_offset.shape, jnp.int32),
+            sem((4,)),
+            sem((points, columns // CHB)), sem, sem,
             sem((half,)), sem((half,)), sem((half,)), sem((half,)),
             sem((half,)), sem((half,)), sem((points,)),
             sem((points,)), sem((points,)), sem((points,)), sem((points,)),
@@ -342,6 +360,14 @@
             transcendentals=0,
         ),
     )(amplitudes, previous, coupling, thresholds, barrier, block_order, window_offset)
+    return pl.pallas_call(
+        write_out,
+        out_shape=jax.ShapeDtypeStruct((points, rows, width), bf16),
+        in_specs=[vmem_spec],
+        out_specs=any_spec,
+        scratch_shapes=[sem((points,))],
+        compiler_params=pltpu.CompilerParams(vmem_limit_bytes=40 << 20),
+    )(staged)
 
 
 def solution(mesh):

time: 61.2 us -> 58 us (0.948)
  local copies, waits for them, and re-layouts: 3.05 us -> 0 us
    unnamed x1 -> x0, local copies, waits for them, and re-layouts: 3.05 us -> none
    pallas_call x1 -> x2, Pallas kernels: 57.4 us -> 57.3 us  [the longest x1 55.9 us: local(): pl.pallas_call(kernel, out_shape=pltpu.VMEM((points, rows, width), bf16),...]
where the time goes in v2:
time: 58 us; the launch traced here: 57.9 us
  Pallas kernels  57.3 us (99%)
  between operations  0.66 us (1%)
    pallas_call x1, Pallas kernels, local(): pl.pallas_call(kernel, out_shape=pltpu.VMEM((points, rows, width), bf16),...  55.9 us
    pallas_call x1, Pallas kernels, local(): pl.pallas_call(write_out, out_shape=jax.ShapeDtypeStruct((points, rows, w...  1.38 us

profile of v2, /device:TPU:97, one launch (start us, length us, event | category | flops | bytes accessed | tf_op | source)
XLA Modules:
  0.0 57.9 jit_solution(11621258796329732076)
XLA Ops:
  0.7 55.9 %shard_map.73.staged = bf16[8,512,256]{2,1,0:T(8,128)(2,1)S(1)} custom-call(bf16[8,512,256]{2,1,0:T(8,128)(2,1)} %amp.1, bf16[8,512,256]{2,1,0:T(8,128)(2,1)} %prev.1, bf16[8,512,2048]{2,1,0:T(8,128)(2,1)} %coup.1, f32[512]{0:T(512)} %thr_in.1, f32[512]{0:T(512)} %bar_in.1, s32[16]{0:T(128)} %order_in.1, s32[1]{0:T(128)S(6)} %copy.8.offset_in), custom_call_target="tpu_custom_call" | custom-call | flops 4294967296 | bytes 23068672 | tf_op jit(solution)/shard_map/pallas_call | solution.py:325
  56.5 1.4 %shard_map.74 = bf16[8,512,256]{2,1,0:T(8,128)(2,1)} custom-call(bf16[8,512,256]{2,1,0:T(8,128)(2,1)S(1)} %shard_map.73.staged), custom_call_target="tpu_custom_call" | custom-call | tf_op jit(solution)/shard_map/pallas_call | solution.py:363

commit v3 on v2

--- a/solution.py
+++ b/solution.py
@@ -9,6 +9,7 @@
 
 CHB = 128
 GRID = 8192
+SPLIT = 2
 MESH = pl.DeviceIdType.MESH
 TAPS = (-205.0 / 72, 8.0 / 5, -1.0 / 5, 8.0 / 315, -1.0 / 560)
 LANES = 128
@@ -30,6 +31,9 @@
     x, yl, z = radial % 4, (radial // 4) % 2, radial // 8
     yh, core = chan // 2, chan % 2
     last = 3
+    pieces = half * SPLIT
+    size = rows // SPLIT
+    far = vecs.at[2]
 
     def at(px, pyl, pz, pyh, pcore):
         return ((pz * 2 + pyl) * 4 + px, pyh * 2 + pcore)
@@ -57,37 +61,47 @@
             src_ref=src, dst_ref=dst, send_sem=send, recv_sem=recv, device_id=to, device_id_type=MESH
         )
 
+    def piece(ref, first, i):
+        row = pl.multiple_of((i % SPLIT) * size, size)
+        return ref.at[first + i // SPLIT, pl.ds(row, size)]
+
     def own_t(i):
-        return remote(amp.at[t_base + i], relay_t.at[i], t_send.at[i], t_recv.at[i], toward)
+        return remote(
+            piece(amp, t_base, i), piece(relay_t, 0, i), t_send, t_recv.at[i], toward
+        )
 
     def own_a(i):
-        return remote(amp.at[a_base + i], relay_a.at[i], a_send.at[i], a_recv.at[i], away)
+        return remote(
+            piece(amp, a_base, i), piece(relay_a, 0, i), a_send, a_recv.at[i], away
+        )
 
     def fwd_t(i):
-        p = t_base + i
-        return remote(relay_t.at[i], vecs.at[2, p], ft_send.at[i], far_recv.at[p], away)
+        landed = far_recv.at[t_base * SPLIT + i]
+        return remote(piece(relay_t, 0, i), piece(far, t_base, i), ft_send, landed, away)
 
     def fwd_a(i):
-        p = a_base + i
-        return remote(relay_a.at[i], vecs.at[2, p], fa_send.at[i], far_recv.at[p], toward)
+        landed = far_recv.at[a_base * SPLIT + i]
+        return remote(piece(relay_a, 0, i), piece(far, a_base, i), fa_send, landed, toward)
 
     def own_sib(p):
-        return remote(amp.at[p], vecs.at[1, p], sib_send.at[p], sib_recv.at[p], sibling)
-
-    def fwd_sib(p):
-        return remote(vecs.at[2, p], vecs.at[3, p], fs_send.at[p], fs_recv.at[p], sibling)
+        return remote(amp.at[p], vecs.at[1, p], sib_send, sib_recv.at[p], sibling)
+
+    def fwd_sib(q):
+        return remote(
+            piece(far, 0, q), piece(vecs.at[3], 0, q), fs_send, fs_recv.at[q], sibling
+        )
 
     def up_own(i):
-        return remote(amp.at[half + i], halo_lo.at[i], up_send.at[i], up_recv.at[i], up_to)
+        return remote(amp.at[half + i], halo_lo.at[i], up_send, up_recv, up_to)
 
     def up_relay(i):
-        return remote(relay_t.at[i], halo_lo.at[i], up_send.at[i], up_recv.at[i], up_to)
+        return remote(relay_t.at[i], halo_lo.at[i], up_send, up_recv, up_to)
 
     def down_own(i):
-        return remote(amp.at[i], halo_hi.at[i], down_send.at[i], down_recv.at[i], down_to)
+        return remote(amp.at[i], halo_hi.at[i], down_send, down_recv, down_to)
 
     def down_relay(i):
-        return remote(relay_t.at[i], halo_hi.at[i], down_send.at[i], down_recv.at[i], down_to)
+        return remote(relay_t.at[i], halo_hi.at[i], down_send, down_recv, down_to)
 
     blocks = coup.shape[2] // CHB
 
@@ -130,9 +144,14 @@
     pl.semaphore_wait(
         barrier, 3 + jnp.where(has_up_to, 1, 0) + jnp.where(has_down_to, 1, 0)
     )
-    for i in range(half):
+
+    def send_own(i, _):
         own_t(i).start()
         own_a(i).start()
+        return 0
+
+    for i in range(pieces):
+        send_own(i, 0)
     for p in range(points):
         own_sib(p).start()
     for i in range(half):
@@ -180,80 +199,125 @@
         for j in range(per):
             columns[k * per + j] = column(s * per + j)
 
-    def product(p, which):
+    def product(p, which, first=0, end=per):
         lhs = jnp.concatenate(
-            [
-                cbuf[p, columns[s * per + j]]
-                for s in which
-                for j in range(per)
-            ],
-            axis=1,
-        )
-        rhs = jnp.concatenate([vecs[s, p] for s in which], axis=0)
+            [cbuf[p, columns[s * per + j]] for s in which for j in range(first, end)], axis=1
+        )
+        part = slice(first * CHB, end * CHB)
+        rhs = jnp.concatenate([vecs[s, p, part, :] for s in which], axis=0)
         return jnp.dot(lhs, rhs, preferred_element_type=jnp.float32)
 
-    def first_hop(i, _):
-        t = own_t(i)
-        t.wait_recv()
-        fwd_t(i).start()
+    def near_product(p, _):
+        own_sib(p).wait_recv()
+        acc[p] = product(p, (0, 1))
+        return 0
+
+    def first_hop(g, _):
+        def pass_on(j, _):
+            i = g * SPLIT + j
+            own_t(i).wait_recv()
+            fwd_t(i).start()
+            own_a(i).wait_recv()
+            fwd_a(i).start()
+            return 0
+
+        lax.fori_loop(0, SPLIT, pass_on, 0)
 
         @pl.when(jnp.logical_and(x == last, has_up_to))
         def _():
-            up_relay(i).start()
+            up_relay(g).start()
 
         @pl.when(jnp.logical_and(x == 0, has_down_to))
         def _():
-            down_relay(i).start()
-
-        own_a(i).wait_recv()
-        fwd_a(i).start()
-
-        def local(q, _):
-            p = i * 2 + q
-            own_sib(p).wait_recv()
-            acc[p] = product(p, (0, 1))
-            return 0
-
-        lax.fori_loop(0, 2, local, 0)
+            down_relay(g).start()
+
         return 0
 
+    lax.fori_loop(0, points, near_product, 0)
     lax.fori_loop(0, half, first_hop, 0)
 
     def arrive(i):
-        for p in (t_base + i, a_base + i):
-            remote(vecs.at[2, p], vecs.at[2, p], ft_send.at[i], far_recv.at[p], away).wait_recv()
-            fwd_sib(p).start()
-
-    def finish(i, write):
-        def one(q, _):
-            p = i + q * half
-            fwd_sib(p).wait_recv()
-            if write:
-                out[p] = ((acc[p] + product(p, (2, 3))) * (1.0 / 3.0)).astype(out.dtype)
-            else:
-                acc[p] += product(p, (2, 3))
+        def one(j, _):
+            for base in (t_base, a_base):
+                q = (base + i) * SPLIT + j
+                here = piece(far, 0, q)
+                remote(here, here, ft_send, far_recv.at[q], away).wait_recv()
+                fwd_sib(q).start()
+            return 0
+
+        lax.fori_loop(0, SPLIT, one, 0)
+
+    def passed(p, first, end):
+        for j in range(first, end):
+            fwd_sib(p * SPLIT + j).wait_recv()
+
+    def finish(i):
+        def one(h, _):
+            p = i + h * half
+            passed(p, 0, SPLIT)
+            acc[p] += product(p, (2, 3))
             return 0
 
         lax.fori_loop(0, 2, one, 0)
+
+    def finish_last(i):
+        early = per - per // SPLIT
+
+        def far_part(h, _):
+            p = i + h * half
+            acc[p] += product(p, (2,))
+            return 0
+
+        def near_part(h, _):
+            p = i + h * half
+            passed(p, 0, SPLIT - 1)
+            acc[p] += product(p, (3,), 0, early)
+            return 0
+
+        def end_part(h, _):
+            p = i + h * half
+            passed(p, SPLIT - 1, SPLIT)
+            total = acc[p] + product(p, (3,), early, per)
+            out[p] = (total * (1.0 / 3.0)).astype(out.dtype)
+            return 0
+
+        lax.fori_loop(0, 2, far_part, 0)
+        far_half = far.at[pl.ds(0, half)]
+        remote(relay_t, far_half, ft_send, far_recv.at[0], away).wait_send()
+        remote(relay_a, far_half, fa_send, far_recv.at[0], toward).wait_send()
+        lax.fori_loop(0, 2, near_part, 0)
+        lax.fori_loop(0, 2, end_part, 0)
 
     def store(i):
         for p in (i, i + half):
             out[p] = (acc[p] * (1.0 / 3.0)).astype(out.dtype)
 
     arrive(0)
-    finish(0, False)
+    finish(0)
     arrive(1)
-    finish(1, False)
+    finish(1)
+
+    first_half = amp.at[pl.ds(0, half)]
 
     @pl.when(has_up_from)
     def _():
-        for i in range(half):
-            up_own(i).wait_recv()
+        remote(first_half, halo_lo, up_send, up_recv, up_to).wait_recv()
 
     @pl.when(has_down_from)
     def _():
-        for i in range(half):
-            down_own(i).wait_recv()
+        remote(first_half, halo_hi, down_send, down_recv, down_to).wait_recv()
+
+    remote(amp, vecs.at[1], sib_send, sib_recv.at[0], sibling).wait_send()
+    remote(first_half, relay_t, t_send, t_recv.at[0], toward).wait_send()
+    remote(first_half, relay_a, a_send, a_recv.at[0], away).wait_send()
+
+    @pl.when(has_up_to)
+    def _():
+        remote(first_half, halo_lo, up_send, up_recv, up_to).wait_send()
+
+    @pl.when(has_down_to)
+    def _():
+        remote(first_half, halo_hi, down_send, down_recv, down_to).wait_send()
 
     prev_copy.wait()
 
@@ -279,28 +343,12 @@
     store(0)
     store(1)
     arrive(2)
-    finish(2, True)
+    finish(2)
+    store(2)
     arrive(3)
-    finish(3, True)
-
-    for i in range(half):
-        own_t(i).wait_send()
-        own_a(i).wait_send()
-        fwd_t(i).wait_send()
-        fwd_a(i).wait_send()
-    for p in range(points):
-        own_sib(p).wait_send()
-        fwd_sib(p).wait_send()
-
-    @pl.when(has_up_to)
-    def _():
-        for i in range(half):
-            up_relay(i).wait_send()
-
-    @pl.when(has_down_to)
-    def _():
-        for i in range(half):
-            down_relay(i).wait_send()
+    finish_last(3)
+
+    remote(far, vecs.at[3], fs_send, fs_recv.at[0], sibling).wait_send()
 
 
 def write_out(staged, out, sems):
@@ -318,6 +366,7 @@
     points, rows, width = amplitudes.shape
     half = points // 2
     columns = coupling.shape[2]
+    pieces = half * SPLIT
     bf16, f32 = jnp.bfloat16, jnp.float32
     sem = pltpu.SemaphoreType.DMA
     any_spec = pl.BlockSpec(memory_space=pl.ANY)
@@ -346,10 +395,10 @@
             pltpu.SMEM(window_offset.shape, jnp.int32),
             sem((4,)),
             sem((points, columns // CHB)), sem, sem,
-            sem((half,)), sem((half,)), sem((half,)), sem((half,)),
-            sem((half,)), sem((half,)), sem((points,)),
-            sem((points,)), sem((points,)), sem((points,)), sem((points,)),
-            sem((half,)), sem((half,)), sem((half,)), sem((half,)),
+            sem, sem((pieces,)), sem, sem((pieces,)),
+            sem, sem, sem((2 * pieces,)),
+            sem, sem((points,)), sem, sem((2 * pieces,)),
+            sem, sem, sem, sem,
         ],
         compiler_params=pltpu.CompilerParams(
             collective_id=0, has_side_effects=True, vmem_limit_bytes=60 << 20

time: 58 us -> 57.2 us (0.986)
  Pallas kernels: 57.3 us -> 56.5 us
    pallas_call x1, Pallas kernels: 55.9 us -> 55.1 us  [local(): pl.pallas_call(kernel, out_shape=pltpu.VMEM((points, rows, width), bf16),...]
where the time goes in v3:
time: 57.2 us; the launch traced here: 57.1 us
  Pallas kernels  56.5 us (99%)
  between operations  0.66 us (1%)
    pallas_call x1, Pallas kernels, local(): pl.pallas_call(kernel, out_shape=pltpu.VMEM((points, rows, width), bf16),...  55.1 us
    pallas_call x1, Pallas kernels, local(): pl.pallas_call(write_out, out_shape=jax.ShapeDtypeStruct((points, rows, w...  1.38 us

profile of v3, /device:TPU:97, one launch (start us, length us, event | category | flops | bytes accessed | tf_op | source)
XLA Modules:
  0.0 57.1 jit_solution(13583652165700461226)
XLA Ops:
  0.7 55.1 %shard_map.73.staged = bf16[8,512,256]{2,1,0:T(8,128)(2,1)S(1)} custom-call(bf16[8,512,256]{2,1,0:T(8,128)(2,1)} %amp.1, bf16[8,512,256]{2,1,0:T(8,128)(2,1)} %prev.1, bf16[8,512,2048]{2,1,0:T(8,128)(2,1)} %coup.1, f32[512]{0:T(512)} %thr_in.1, f32[512]{0:T(512)} %bar_in.1, s32[16]{0:T(128)} %order_in.1, s32[1]{0:T(128)S(6)} %copy.8.offset_in), custom_call_target="tpu_custom_call" | custom-call | flops 4294967296 | bytes 23068672 | tf_op jit(solution)/shard_map/pallas_call | solution.py:374
  55.7 1.4 %shard_map.74 = bf16[8,512,256]{2,1,0:T(8,128)(2,1)} custom-call(bf16[8,512,256]{2,1,0:T(8,128)(2,1)S(1)} %shard_map.73.staged), custom_call_target="tpu_custom_call" | custom-call | tf_op jit(solution)/shard_map/pallas_call | solution.py:412

commit v4 on v3

--- a/solution.py
+++ b/solution.py
@@ -28,8 +28,8 @@
     half = points // 2
     per = rows // CHB
     radial, chan = lax.axis_index("radial"), lax.axis_index("chan")
-    x, yl, z = radial % 4, (radial // 4) % 2, radial // 8
-    yh, core = chan // 2, chan % 2
+    x, yl, z = lax.rem(radial, 4), lax.rem(lax.div(radial, 4), 2), lax.div(radial, 8)
+    yh, core = lax.div(chan, 2), lax.rem(chan, 2)
     last = 3
     pieces = half * SPLIT
     size = rows // SPLIT
@@ -42,16 +42,16 @@
     away = at(x, 1 - yl, z, 1 - yh, core)
     sibling = at(x, yl, z, yh, 1 - core)
     up_z = jnp.where(x == last, z + (1 - yl), z)
-    up_to = at((x + 1) % 4, yl, jnp.minimum(up_z, 3), yh, core)
+    up_to = at(lax.rem(x + 1, 4), yl, jnp.minimum(up_z, 3), yh, core)
     has_up_to = up_z <= 3
     down_z = jnp.where(x == 0, z - yl, z)
-    down_to = at((x + 3) % 4, yl, jnp.maximum(down_z, 0), yh, core)
+    down_to = at(lax.rem(x + 3, 4), yl, jnp.maximum(down_z, 0), yh, core)
     has_down_to = down_z >= 0
     up_fz = jnp.where(x == 0, z - (1 - yl), z)
-    up_from = at((x + 3) % 4, yl, jnp.maximum(up_fz, 0), yh, core)
+    up_from = at(lax.rem(x + 3, 4), yl, jnp.maximum(up_fz, 0), yh, core)
     has_up_from = up_fz >= 0
     down_fz = jnp.where(x == last, z + yl, z)
-    down_from = at((x + 1) % 4, yl, jnp.minimum(down_fz, 3), yh, core)
+    down_from = at(lax.rem(x + 1, 4), yl, jnp.minimum(down_fz, 3), yh, core)
     has_down_from = down_fz <= 3
     t_base = jnp.where(x < 2, 0, half)
     a_base = half - t_base
@@ -127,16 +127,16 @@
     prev_copy = pltpu.make_async_copy(prev, pbuf, prev_sem)
 
     barrier = pltpu.get_barrier_semaphore()
+    @pl.when(has_up_from)
+    def _():
+        pl.semaphore_signal(barrier, inc=1, device_id=up_from, device_id_type=MESH)
+
+    @pl.when(has_down_from)
+    def _():
+        pl.semaphore_signal(barrier, inc=1, device_id=down_from, device_id_type=MESH)
+
     for to in (toward, away, sibling):
         pl.semaphore_signal(barrier, inc=1, device_id=to, device_id_type=MESH)
-
-    @pl.when(has_up_from)
-    def _():
-        pl.semaphore_signal(barrier, inc=1, device_id=up_from, device_id_type=MESH)
-
-    @pl.when(has_down_from)
-    def _():
-        pl.semaphore_signal(barrier, inc=1, device_id=down_from, device_id_type=MESH)
 
     own_copy.start()
     for copy in small:
@@ -349,17 +349,6 @@
     finish_last(3)
 
     remote(far, vecs.at[3], fs_send, fs_recv.at[0], sibling).wait_send()
-
-
-def write_out(staged, out, sems):
-    copies = [
-        pltpu.make_async_copy(staged.at[p], out.at[p], sems.at[p])
-        for p in range(staged.shape[0])
-    ]
-    for copy in copies:
-        copy.start()
-    for copy in copies:
-        copy.wait()
 
 
 def local(amplitudes, previous, coupling, thresholds, barrier, block_order, window_offset):
@@ -409,14 +398,7 @@
             transcendentals=0,
         ),
     )(amplitudes, previous, coupling, thresholds, barrier, block_order, window_offset)
-    return pl.pallas_call(
-        write_out,
-        out_shape=jax.ShapeDtypeStruct((points, rows, width), bf16),
-        in_specs=[vmem_spec],
-        out_specs=any_spec,
-        scratch_shapes=[sem((points,))],
-        compiler_params=pltpu.CompilerParams(vmem_limit_bytes=40 << 20),
-    )(staged)
+    return staged
 
 
 def solution(mesh):

time: 57.2 us -> 57.1 us (level)
  Pallas kernels: 56.5 us -> 55 us
  local copies, waits for them, and re-layouts: 0 us -> 1.32 us
    pallas_call x1 -> x0, Pallas kernels: 1.38 us -> none  [local(): pl.pallas_call(write_out, out_shape=jax.ShapeDtypeStruct((points, rows, w...]
    unnamed x0 -> x1, local copies, waits for them, and re-layouts: none -> 1.32 us
where the time goes in v4:
time: 57.1 us; the launch traced here: 57 us
  Pallas kernels  55 us (96%)
  local copies, waits for them, and re-layouts  1.32 us (2%)
  between operations  0.66 us (1%)
    pallas_call x1, Pallas kernels, local(): pl.pallas_call(kernel, out_shape=pltpu.VMEM((points, rows, width), bf16),...  55 us
    unnamed x1, local copies, waits for them, and re-layouts  1.32 us

profile of v4, /device:TPU:97, one launch (start us, length us, event | category | flops | bytes accessed | tf_op | source)
XLA Modules:
  0.0 57.0 jit_solution(8750704778248952664)
XLA Ops:
  0.7 55.0 %shard_map.73 = bf16[8,512,256]{2,1,0:T(8,128)(2,1)S(1)} custom-call(bf16[8,512,256]{2,1,0:T(8,128)(2,1)} %amp.1, bf16[8,512,256]{2,1,0:T(8,128)(2,1)} %prev.1, bf16[8,512,2048]{2,1,0:T(8,128)(2,1)} %coup.1, f32[512]{0:T(512)} %thr_in.1, f32[512]{0:T(512)} %bar_in.1, s32[16]{0:T(128)} %order_in.1, s32[1]{0:T(128)S(6)} %copy.10.offset_in), custom_call_target="tpu_custom_call" | custom-call | flops 4294967296 | bytes 23068672 | tf_op jit(solution)/shard_map/pallas_call | solution.py:363
  55.7 1.3 %copy.9 = bf16[8,512,256]{2,1,0:T(8,128)(2,1)} copy(bf16[8,512,256]{2,1,0:T(8,128)(2,1)S(1)} %shard_map.73) | data formatting | bytes 4194304
